TPU v7x, 32 devices: a whole 2x2x4 slice. The times are simulated.
32 devices in a mesh: parts: 2 (over y), dp: 8 (over z, x), tensor: 2 (over core).
Axes of the slice: x: 2, y: 2, z: 4, core: 2. Of those that a mesh axis runs over, the one named last changes fastest.
Arguments:
- activations: bfloat16 [2, 8192, 25600], P(None, ('parts', 'dp'), 'tensor'), parts along dimension 1, may hold values from -6 to 6
- out_grads: bfloat16 [2, 8192, 5120], P(None, ('parts', 'dp'), 'tensor'), parts along dimension 1, may hold values from -6 to 6
- proj_in: bfloat16 [25600, 64], P('tensor'), may hold values from -0.0390625 to 0.0390625
- proj_out: bfloat16 [5120, 64], P('tensor'), may hold values from -0.078125 to 0.078125
- token_ids: int32 [32, 256], P(('parts', 'dp')), parts along dimension 0, may hold values from 0 to 151643, as said below
- queries: bfloat16 [2, 2048, 4096], P(None, 'tensor', 'dp'), may hold values from -6 to 6
- query_docs: int32 [4096, 8], P(('parts', 'tensor')), parts along dimension 0, may hold values from 0 to 15, all different within a row
Outputs:
- scores: float32 [32, 2048], P(('parts', 'dp'), 'tensor'), parts along dimension 0
- listed: float32 [4096], P(('parts', 'tensor')), parts along dimension 0
There are 2 independent parts, one for each index of `parts`. A program takes and returns all parts, laid end to end along the dimension named above; an argument that names none is the same for every part. Nothing has to cross between parts.
Inputs may be any that keep to these rules, and one draw needn't show every extreme that they name: `token_ids`: each document is a run of real token ids below 151643 followed by padding id 151643 up to its end; it has at least 64 real tokens, and some document is padded. `query_docs`: each query lists 8 different documents.
All inputs are finite; a program needn't handle non-finite values.
Results may differ from a plain program's by a relative error of at most 0.0029.
Values may be sent and summed in bfloat16 or wider, within the bound.
No kernel may reach another device: no remote copies, remote signals or barrier semaphores. Data moves between devices by JAX's collectives and lax.ppermute only.
A program may use at most 128 MiB of HBM per device.

v0:
```python
import jax
import jax.numpy as jnp
from jax import lax
from jax.sharding import PartitionSpec as P

R = 64
K = 8


pad_token = 151643


def body(activations, out_grads, proj_in, proj_out, token_ids, queries, query_docs):
    checkpoints = activations.shape[0]
    rank_size = proj_in.shape[1]
    docs_here, doc_len = token_ids.shape
    in_part = jnp.einsum("ctf,fr->ctr", activations, proj_in, preferred_element_type=jnp.float32)
    out_part = jnp.einsum("ctd,dr->ctr", out_grads, proj_out, preferred_element_type=jnp.float32)
    in_proj, out_proj = lax.psum((in_part, out_part), "tensor")
    keep_mask = (token_ids != pad_token).astype(jnp.float32).reshape(1, docs_here, doc_len, 1)
    in_proj = in_proj.reshape(checkpoints, docs_here, doc_len, rank_size)
    out_proj = out_proj.reshape(checkpoints, docs_here, doc_len, rank_size) * keep_mask
    doc_sums = jnp.einsum("cntr,cnts->cnrs", out_proj, in_proj, precision=lax.Precision.HIGHEST)
    doc_grads = (
        (doc_sums * doc_len ** (-0.5))
        .reshape(checkpoints, docs_here, rank_size * rank_size)
        .astype(jnp.bfloat16)
    )
    summed = jnp.einsum(
        "cnf,cqf->nq",
        doc_grads,
        lax.all_gather(queries, "dp", axis=2, tiled=True),
        preferred_element_type=jnp.float32,
    )
    scores = summed / R
    doc_index = lax.axis_index("dp") * docs_here + jnp.arange(docs_here, dtype=jnp.int32)
    matches = (query_docs[:, :, None] == doc_index[None, None, :]).astype(jnp.float32)
    own_terms = jnp.einsum("qkn,nq->q", matches, scores)
    listed = lax.psum(own_terms, "dp") / K
    return (scores, listed)


def solution(mesh):
    in_specs = (
        P(None, ("parts", "dp"), "tensor"),
        P(None, ("parts", "dp"), "tensor"),
        P("tensor", None),
        P("tensor", None),
        P(("parts", "dp"), None),
        P(None, "tensor", "dp"),
        P(("parts", "tensor"), None),
    )
    out_specs = (P(("parts", "dp"), "tensor"), P(("parts", "tensor")))
    return jax.shard_map(body, mesh=mesh, in_specs=in_specs, out_specs=out_specs, check_vma=False)
```

profile of v0, /device:TPU:0, one launch (start us, length us, event | category | flops | bytes accessed | tf_op | source)
XLA Modules:
  0.0 296.3 jit_solution(15274263244445660772)
XLA Ops:
  8.0 0.0 copy-start
  8.0 0.0 all-reduce.3.cloned.1.call-start
  8.1 4.3 %fusion.4 = f32[2,512,64]{1,2,0:T(8,128)S(1)} fusion(bf16[2,512,2560]{2,1,0:T(8,128)(2,1)} %param.8, bf16[2560,64]{0,1:T(8,128)(2,1)} %param.10), kind=kOutput, calls=%fused_computation.6 | convolution fusion | flops 335544320 | bytes 5832704 | tf_op jit(solution)/shard_map/ctd,dr->ctr/dot_general | solution.py:18
  12.4 0.0 copy-done
  12.4 0.0 copy-start.1
  12.4 0.0 copy-start.2
  12.4 12.8 %fusion = f32[2,512,64]{1,2,0:T(8,128)S(1)} fusion(bf16[2,512,12800]{2,1,0:T(8,128)(2,1)} %param.7, bf16[12800,64]{0,1:T(8,128)(2,1)S(1)} %copy-done), kind=kOutput, calls=%fused_computation | convolution fusion | flops 1677721600 | bytes 28114944 | tf_op jit(solution)/shard_map/ctf,fr->ctr/dot_general | solution.py:17
  25.2 0.8 copy_bitcast_fusion
  26.1 0.0 all-reduce.3.cloned.1.call-update
  26.1 0.0 all-gather.2.cloned.1.call-start
  26.2 0.5 all-gather.2.cloned.1.call-update
  26.7 0.0 copy-done.1
  26.7 0.1 convert_reduce_fusion
  26.8 0.0 copy-done.2
  26.8 20.9 %all-reduce.3.cloned.1.call-done = (f32[2,2,256,64]{2,3,1,0:T(8,128)}, f32[2,2,256,64]{2,3,1,0:T(8,128)}) async-done(((f32[2,2,256,64]{2,3,1,0:T(8,128)}, f32[2,2,256,64]{2,3,1,0:T(8,128)}), (f32[2,2,256,64]{2,3,1,0:T(8,128)}, f32[2,2,256,64]{2,3,1,0:T(8,128)})) %all-reduce.3.cloned.1.call-update) | async-done | bytes 524304 | tf_op jit(solution)/shard_map/psum | solution.py:19
  47.7 1.4 fusion.2
  49.2 0.1 convert_element_type.14
  49.3 209.6 %all-gather.2.cloned.1.call-done = bf16[2,1024,4096]{2,1,0:T(8,128)(2,1)} async-done(((bf16[2,1024,512]{2,1,0:T(8,128)(2,1)}), bf16[2,1024,4096]{2,1,0:T(8,128)(2,1)}) %all-gather.2.cloned.1.call-update) | async-done | bytes 16777232 | tf_op jit(solution)/shard_map/all_gather | solution.py:32
  258.9 10.8 %multiply_reduce_fusion = (f32[1024]{0:T(1024)S(1)}, f32[2,1024]{1,0:T(2,128)}) fusion(f32[1024,2]{0,1:T(2,128)S(1)} %convert_reduce_fusion, bf16[2,2,4096]{2,1,0:T(2,128)(2,1)S(1)} %convert_element_type.14, bf16[2,1024,4096]{2,1,0:T(8,128)(2,1)} %all-gather.2.cloned.1.call-done), kind=kOutput, calls=%fused_computation.13 | convolution fusion | flops 33559552 | bytes 16830464 | tf_op jit(solution)/shard_map/cnf,cqf->nq/dot_general | solution.py:29
  269.7 18.6 %psum.23 = f32[1024]{0:T(1024)S(1)} all-reduce(f32[1024]{0:T(1024)S(1)} %get-tuple-element.4), channel_id=1, replica_groups=mesh['parts'=2,'dp'=8,'tensor'=2] {'dp'}, use_global_device_ids=true, to_apply=%region_3.0 | all-reduce | flops 1024 | bytes 8192 | tf_op jit(solution)/shard_map/psum | solution.py:39
  288.3 0.6 broadcast_multiply_fusion
  (2 shorter events, 0.0 us)
Async XLA Ops:
  8.0 4.4 %copy-start = (bf16[12800,64]{0,1:T(8,128)(2,1)S(1)}, bf16[12800,64]{0,1:T(8,128)(2,1)}, u32[]{:S(2)}) copy-start(bf16[12800,64]{0,1:T(8,128)(2,1)} %param.9) | copy-start | bytes 4915204
  8.0 39.7 %all-reduce.3.cloned.1.call-start = ((), (), s32[]{:S(2)}) async-start(), calls=%async_computation.1 | async-start | bytes 1048576 | tf_op jit(solution)/shard_map/psum | solution.py:19
  12.4 14.3 %copy-start.1 = (s32[1024,8]{0,1:T(8,128)S(1)}, s32[1024,8]{0,1:T(8,128)}, u32[]{:S(2)}) copy-start(s32[1024,8]{0,1:T(8,128)} %param.13) | copy-start | bytes 98308
  12.4 14.4 %copy-start.2 = (s32[2,256]{1,0:T(2,128)S(1)}, s32[2,256]{1,0:T(2,128)}, u32[]{:S(2)}) copy-start(s32[2,256]{1,0:T(2,128)} %param.11) | copy-start | bytes 6148
  26.1 232.8 %all-gather.2.cloned.1.call-start = ((), (), s32[]{:S(2)}) async-start(), calls=%async_computation | async-start | bytes 18874368 | tf_op jit(solution)/shard_map/all_gather | solution.py:32
Sparse Core Ops, SparseCore 0:
  26.2 21.4 all-reduce.2
Sparse Core Ops, SparseCore 1:
  28.8 230.0 all-gather.1
where the time goes:
time: 297 us; the launch traced here: 296 us
  waiting for transfers between devices  231 us (78%)
  matrix products  29.4 us (10%)
  blocking collectives  18.6 us (6%)
  between operations  15.6 us (5%)
    all_gather x1, waiting for transfers between devices, body(): lax.all_gather(queries, 'dp', axis=2, tiled=True)  210 us
    psum x1, waiting for transfers between devices, body(): in_proj, out_proj = lax.psum((in_part, out_part), 'tensor')  20.9 us
    psum x1, blocking collectives, body(): listed = lax.psum(own_terms, 'dp') / K  18.6 us
    dot_general x1, matrix products, body(): jnp.einsum('ctf,fr->ctr', activations, proj_in, preferred_element_type=jn...  12.8 us
    dot_general x1, matrix products, body(): jnp.einsum('cnf,cqf->nq', doc_grads, lax.all_gather(queries, 'dp', axis=2...  10.8 us
  transfers between devices with their start and end apart: 2, of which 2 were waited for; matrix products, arithmetic and copies ran while one was open for 1% of the time, Pallas kernels for 0%

commit v1 on v0

v1 whole, which is shorter than its diff:
```python
import jax
import jax.numpy as jnp
from jax import lax
from jax.sharding import PartitionSpec as P

PAD = 151643


def sum_over_tensor(part, size):
    if size == 2:
        return part + lax.ppermute(part, "tensor", [(0, 1), (1, 0)])
    return lax.psum(part, "tensor")


def body(dp, tensor, activations, out_grads, proj_in, proj_out, token_ids, queries, query_docs):
    checkpoints = activations.shape[0]
    rank = proj_in.shape[1]
    docs, doc_len = token_ids.shape
    rows = rank // dp
    own_queries = queries.shape[1]

    out_part = jnp.einsum("ctd,dr->ctr", out_grads, proj_out, preferred_element_type=jnp.float32)
    out_proj = sum_over_tensor(out_part, tensor)
    in_part = jnp.einsum("ctf,fr->ctr", activations, proj_in, preferred_element_type=jnp.float32)
    keep = (token_ids != PAD).astype(jnp.float32).reshape(1, docs, doc_len, 1)
    out_proj = out_proj.reshape(checkpoints, docs, doc_len, rank) * keep
    in_part = in_part.reshape(checkpoints, docs, doc_len, rank)
    term = jnp.einsum("cntr,cnts->crns", out_proj, in_part, precision=lax.Precision.HIGHEST)
    term = term.reshape(checkpoints, dp, 1, rows, docs * rank).transpose(1, 2, 0, 3, 4)
    term = jnp.broadcast_to(term, (dp, tensor, checkpoints, rows, docs * rank))
    term = term.reshape(dp * tensor, checkpoints, rows, docs * rank)
    terms = lax.all_to_all(term, ("dp", "tensor"), 0, 0, tiled=True)
    grads = terms.reshape(dp, tensor, checkpoints, rows, docs, rank).sum(1) * doc_len ** (-0.5)
    grads = grads.astype(jnp.bfloat16).transpose(1, 0, 3, 2, 4).reshape(checkpoints, dp * docs, rows * rank)

    part = jnp.einsum("cnf,cqf->nq", grads, queries, preferred_element_type=jnp.float32)
    every_doc = jnp.arange(dp * docs, dtype=jnp.int32)
    listing = (query_docs.T[None] == every_doc[:, None, None]).sum(1).astype(jnp.float32)
    listed_part = (listing * part).sum(0)
    sent = jnp.concatenate(
        [
            part.reshape(dp, docs, own_queries),
            jnp.broadcast_to(listed_part, (dp, 1, own_queries)),
        ],
        axis=1,
    )
    total = lax.all_to_all(sent, "dp", 0, 0, tiled=True).sum(0) / rank
    return total[:docs], total[docs] / query_docs.shape[1]


def solution(mesh):
    dp, tensor = mesh.shape["dp"], mesh.shape["tensor"]
    in_specs = (
        P(None, ("parts", "dp"), "tensor"),
        P(None, ("parts", "dp"), "tensor"),
        P("tensor", None),
        P("tensor", None),
        P(("parts", "dp"), None),
        P(None, "tensor", "dp"),
        P(("parts", "tensor"), None),
    )
    out_specs = (P(("parts", "dp"), "tensor"), P(("parts", "tensor")))
    return jax.shard_map(
        lambda *arrays: body(dp, tensor, *arrays),
        mesh=mesh,
        in_specs=in_specs,
        out_specs=out_specs,
        check_vma=False,
    )
```

time: 297 us -> 47.3 us (0.16)
  waiting for transfers between devices: 231 us -> 7.76 us
  between operations: 15.6 us -> 0.81 us
  matrix products: 29.4 us -> 18.2 us
  blocking collectives: 18.6 us -> 9.74 us
  starting transfers between devices: 0.08 us -> 7.54 us
    all_gather x1 -> x0, waiting for transfers between devices: 210 us -> none  [body(): lax.all_gather(queries, 'dp', axis=2, tiled=True)]
    psum x1 -> x0, waiting for transfers between devices: 20.9 us -> none  [body(): in_proj, out_proj = lax.psum((in_part, out_part), 'tensor')]
    psum x1 -> x0, blocking collectives: 18.6 us -> none  [body(): listed = lax.psum(own_terms, 'dp') / K]
    dot_general x2, matrix products: 12.2 us -> 1.05 us  [the longest x1 0.66 us: body(): jnp.einsum('cnf,cqf->nq', grads, queries, preferred_element_type=jnp.floa...]
    all_to_all x0 -> x1, blocking collectives: none -> 9.74 us  [body(): total = lax.all_to_all(sent, 'dp', 0, 0, tiled=True).sum(0) / rank]
    all_to_all x0 -> x1, waiting for transfers between devices: none -> 7.76 us  [body(): terms = lax.all_to_all(term, ('dp', 'tensor'), 0, 0, tiled=True)]
    all_to_all x0 -> x1, starting transfers between devices: none -> 7.02 us  [body(): terms = lax.all_to_all(term, ('dp', 'tensor'), 0, 0, tiled=True)]
  transfers between devices with their start and end apart: 2 -> 2, of which waited for: 2 -> 1; matrix products, arithmetic and copies ran while one was open for 1% -> 28% of each run, Pallas kernels for 0% -> 0%
where the time goes in v1:
time: 47.3 us; the launch traced here: 47.1 us
  matrix products  18.2 us (38%)
  blocking collectives  9.74 us (21%)
  waiting for transfers between devices  7.76 us (16%)
  starting transfers between devices  7.54 us (16%)
  local copies, waits for them, and re-layouts  1.9 us (4%)
  other arithmetic  1.12 us (2%)
  between operations  0.81 us (2%)
    dot_general x1, matrix products, body(): jnp.einsum('ctf,fr->ctr', activations, proj_in, preferred_element_type=jn...  12.8 us
    all_to_all x1, blocking collectives, body(): total = lax.all_to_all(sent, 'dp', 0, 0, tiled=True).sum(0) / rank  9.74 us
    all_to_all x1, waiting for transfers between devices, body(): terms = lax.all_to_all(term, ('dp', 'tensor'), 0, 0, tiled=True)  7.76 us
    all_to_all x1, starting transfers between devices, body(): terms = lax.all_to_all(term, ('dp', 'tensor'), 0, 0, tiled=True)  7.02 us
    dot_general x1, matrix products, body(): jnp.einsum('ctd,dr->ctr', out_grads, proj_out, preferred_element_type=jnp...  4.36 us
  transfers between devices with their start and end apart: 2, of which 1 were waited for; matrix products, arithmetic and copies ran while one was open for 28% of the time, Pallas kernels for 0%

profile of v1, /device:TPU:0, one launch (start us, length us, event | category | flops | bytes accessed | tf_op | source)
XLA Modules:
  0.0 47.1 jit_solution(16803881787594143903)
XLA Ops:
  0.6 0.0 copy-start
  0.6 0.0 copy-start.1
  0.7 4.4 %fusion.2 = f32[2,512,64]{1,2,0:T(8,128)S(1)} fusion(bf16[2,512,2560]{2,1,0:T(8,128)(2,1)} %param.8, bf16[2560,64]{0,1:T(8,128)(2,1)} %param.10), kind=kOutput, calls=%fused_computation.6 | convolution fusion | flops 335544320 | bytes 5832704 | tf_op jit(solution)/shard_map/ctd,dr->ctr/dot_general | solution.py:22
  5.0 0.0 copy-start.3
  5.0 0.0 copy-start.2
  5.0 0.5 %collective-permute-start = (f32[2,512,64]{1,2,0:T(8,128)S(1)}, f32[2,512,64]{1,2,0:T(8,128)S(1)}, u32[]{:S(2)}, u32[]{:S(2)}) collective-permute-start(f32[2,512,64]{1,2,0:T(8,128)S(1)} %fusion.2), channel_id=1, source_target_pairs={{0,1},{1,0},{2,3},{3,2},{4,5},{5,4},{6,7},{7,6},{8,9},{9,8},{10,11... | collective-permute-start | bytes 786440 | tf_op jit(solution)/shard_map/ppermute | solution.py:11
  5.6 0.0 copy-done.1
  5.6 12.8 %fusion = f32[2,512,64]{1,2,0:T(8,128)S(1)} fusion(bf16[2,512,12800]{2,1,0:T(8,128)(2,1)} %param.7, bf16[12800,64]{0,1:T(8,128)(2,1)S(1)} %copy-done.1), kind=kOutput, calls=%fused_computation | convolution fusion | flops 1677721600 | bytes 28114944 | tf_op jit(solution)/shard_map/ctf,fr->ctr/dot_general | solution.py:24
  18.4 0.0 copy-done.3
  18.4 0.0 collective-permute-done
  18.5 0.4 convolution_bitcast_fusion
  18.9 0.1 copy.22
  19.0 0.1 reshape.32
  19.1 0.7 %broadcast_in_dim.13 = f32[8,2,2,8,128]{4,3,2,1,0:T(8,128)} broadcast(f32[8,2,8,128]{3,2,1,0:T(8,128)S(1)} %copy.23), dimensions={0,2,3,4} | broadcast | bytes 196608 | tf_op jit(solution)/shard_map/broadcast_in_dim | solution.py:30
  19.8 7.0 %all-to-all-start = ((f32[16,2,8,128]{3,2,1,0:T(8,128)}), f32[16,2,8,128]{3,2,1,0:T(8,128)S(1)}, u32[]{:S(2)}, u32[]{:S(2)}) async-start(f32[16,2,8,128]{3,2,1,0:T(8,128)} %bitcast.5), calls=%async_computation | async-start | bytes 262144 | tf_op jit(solution)/shard_map/all_to_all | solution.py:32
  26.8 0.0 copy-done.2
  26.8 0.2 convert_reduce_fusion
  27.0 7.8 %all-to-all-done = f32[16,2,8,128]{3,2,1,0:T(8,128)S(1)} async-done(((f32[16,2,8,128]{3,2,1,0:T(8,128)}), f32[16,2,8,128]{3,2,1,0:T(8,128)S(1)}, u32[]{:S(2)}, u32[]{:S(2)}) %all-to-all-start) | async-done | bytes 131104 | tf_op jit(solution)/shard_map/all_to_all | solution.py:32
  34.7 0.2 reshape.34
  34.9 0.2 reduce_sum.36
  35.2 0.1 reshape.35
  35.3 0.0 copy-done
  35.3 0.7 %multiply_reduce_fusion = (f32[1024]{0:T(1024)S(1)}, f32[16,1024]{1,0:T(8,128)S(1)}) fusion(s32[16,1024]{1,0:T(8,128)S(1)} %convert_reduce_fusion, bf16[2,16,512]{2,1,0:T(8,128)(2,1)S(1)} %reshape.35, bf16[2,1024,512]{2,1,0:T(8,128)(2,1)S(1)} %copy-done), kind=kOutput, calls=%fused_computation.17 | convolution fusion | flops 33602560 | bytes 2265088 | tf_op jit(solution)/shard_map/cnf,cqf->nq/dot_general | solution.py:36
  36.0 0.1 pad_maximum_fusion
  36.1 9.7 %all_to_all.10 = f32[8,3,1024]{2,1,0:T(4,128)S(1)} all-to-all(f32[8,3,1024]{2,1,0:T(4,128)S(1)} %pad_maximum_fusion), channel_id=1, replica_groups=mesh['parts'=2,'dp'=8,'tensor'=2] {'dp'}, dimensions={0} | all-to-all | bytes 196608 | tf_op jit(solution)/shard_map/all_to_all | solution.py:47
  45.9 0.6 %slice.8 = f32[2,1024]{1,0:T(2,128)} slice(f32[3,1024]{1,0:T(4,128)S(1)} %broadcast_multiply_fusion), slice={[0:2], [0:1024]} | slice | bytes 16384 | tf_op jit(solution)/shard_map/slice | solution.py:48
  46.5 0.6 %slice_multiply_fusion = f32[1,1024]{1,0:T(1,128)} fusion(f32[3,1024]{1,0:T(4,128)S(1)} %broadcast_multiply_fusion), kind=kLoop, calls=%fused_computation.19 | loop fusion | flops 1024 | bytes 8192 | tf_op jit(solution)/shard_map/div | solution.py:48
  (9 shorter events, 0.2 us)
Async XLA Ops:
  0.6 34.7 %copy-start = (bf16[2,1024,512]{2,1,0:T(8,128)(2,1)S(1)}, bf16[2,1024,512]{2,1,0:T(8,128)(2,1)}, u32[]{:S(2)}) copy-start(bf16[2,1024,512]{2,1,0:T(8,128)(2,1)} %param.12) | copy-start | bytes 6291460
  0.6 4.9 %copy-start.1 = (bf16[12800,64]{0,1:T(8,128)(2,1)S(1)}, bf16[12800,64]{0,1:T(8,128)(2,1)}, u32[]{:S(2)}) copy-start(bf16[12800,64]{0,1:T(8,128)(2,1)} %param.9) | copy-start | bytes 4915204
  5.0 13.4 %copy-start.3 = (s32[2,256]{1,0:T(2,128)S(1)}, s32[2,256]{1,0:T(2,128)}, u32[]{:S(2)}) copy-start(s32[2,256]{1,0:T(2,128)} %param.11) | copy-start | bytes 6148
  5.0 21.8 %copy-start.2 = (s32[1024,8]{0,1:T(8,128)S(1)}, s32[1024,8]{0,1:T(8,128)}, u32[]{:S(2)}) copy-start(s32[1024,8]{0,1:T(8,128)} %param.13) | copy-start | bytes 98308
  5.0 13.4 %collective-permute-start = (f32[2,512,64]{1,2,0:T(8,128)S(1)}, f32[2,512,64]{1,2,0:T(8,128)S(1)}, u32[]{:S(2)}, u32[]{:S(2)}) collective-permute-start(f32[2,512,64]{1,2,0:T(8,128)S(1)} %fusion.2), channel_id=1, source_target_pairs={{0,1},{1,0},{2,3},{3,2},{4,5},{5,4},{6,7},{7,6},{8,9},{9,8},{10,11... | collective-permute-start | bytes 786440 | tf_op jit(solution)/shard_map/ppermute | solution.py:11
  19.8 15.0 %all-to-all-start = ((f32[16,2,8,128]{3,2,1,0:T(8,128)}), f32[16,2,8,128]{3,2,1,0:T(8,128)S(1)}, u32[]{:S(2)}, u32[]{:S(2)}) async-start(f32[16,2,8,128]{3,2,1,0:T(8,128)} %bitcast.5), calls=%async_computation | async-start | bytes 262144 | tf_op jit(solution)/shard_map/all_to_all | solution.py:32

commit v2 on v1

--- a/solution.py
+++ b/solution.py
@@ -1,9 +1,197 @@
+import functools
+
 import jax
 import jax.numpy as jnp
 from jax import lax
+from jax.experimental import pallas as pl
+from jax.experimental.pallas import tpu as pltpu
 from jax.sharding import PartitionSpec as P
 
 PAD = 151643
+BLOCK = 128
+VMEM = pl.BlockSpec(memory_space=pltpu.VMEM)
+HBM = pl.BlockSpec(memory_space=pltpu.HBM)
+LAST = (((1,), (1,)), ((), ()))
+
+
+def project_kernel(
+    doc_len, acts_ref, outs_ref, in_ref, out_ref, mine_ref, theirs_ref, acts, outs, infac, outfac, act_sems, out_sems, fac_sems
+):
+    checkpoints, tokens, _ = acts.shape
+    rank = infac.shape[0]
+    half = checkpoints * rank
+    steps = tokens // BLOCK
+    keeps = lax.axis_index("tensor")
+
+    def rows_of(i):
+        return pl.ds(pl.multiple_of(i * BLOCK, BLOCK), BLOCK)
+
+    def out_copy(i, c):
+        return pltpu.make_async_copy(outs_ref.at[c, rows_of(i)], outs.at[c, rows_of(i)], out_sems.at[i, c])
+
+    def act_copy(i, c):
+        return pltpu.make_async_copy(acts_ref.at[c, rows_of(i)], acts.at[c, rows_of(i)], act_sems.at[i, c])
+
+    out_fac_copy = pltpu.make_async_copy(out_ref, outfac, fac_sems.at[0])
+    in_fac_copy = pltpu.make_async_copy(in_ref, infac, fac_sems.at[1])
+
+    def start_outs(i, carry):
+        for c in range(checkpoints):
+            out_copy(i, c).start()
+        return carry
+
+    def start_acts(i, carry):
+        for c in range(checkpoints):
+            act_copy(i, c).start()
+        return carry
+
+    out_fac_copy.start()
+    lax.fori_loop(0, steps, start_outs, 0)
+    in_fac_copy.start()
+    lax.fori_loop(0, steps, start_acts, 0)
+
+    def project(i, copy, wide, factor, side):
+        for c in range(checkpoints):
+            copy(i, c).wait()
+        found = [
+            lax.dot_general(wide[c, rows_of(i)], factor[...], LAST, preferred_element_type=jnp.float32)
+            for c in range(checkpoints)
+        ]
+        both = jnp.concatenate(found, axis=1)
+        doc = i // (doc_len // BLOCK)
+        at = pl.ds(pl.multiple_of(i * BLOCK - doc * doc_len, BLOCK), BLOCK)
+
+        @pl.when(doc == keeps)
+        def _():
+            mine_ref[at, side * half : (side + 1) * half] = both
+
+        @pl.when(doc != keeps)
+        def _():
+            theirs_ref[at, side * half : (side + 1) * half] = both
+
+    def out_step(i, carry):
+        project(i, out_copy, outs, outfac, 0)
+        return carry
+
+    def act_step(i, carry):
+        project(i, act_copy, acts, infac, 1)
+        return carry
+
+    out_fac_copy.wait()
+    lax.fori_loop(0, steps, out_step, 0)
+    in_fac_copy.wait()
+    lax.fori_loop(0, steps, act_step, 0)
+
+
+def grad_kernel(dp, tensor, checkpoints, ids_ref, mine_ref, other_ref, sent_ref):
+    doc_len = mine_ref.shape[0]
+    half = mine_ref.shape[1] // 2
+    rank = half // checkpoints
+    rows = rank // dp
+    ids = ids_ref[pl.ds(lax.axis_index("tensor"), 1), :]
+    keep = jnp.where(ids != PAD, doc_len**-0.5, 0.0)
+    both = mine_ref[...] + other_ref[...]
+    kept = both[:, :half].T * keep
+    sums = jnp.dot(
+        kept, both[:, half:], precision=lax.Precision.HIGHEST, preferred_element_type=jnp.float32
+    )
+    grads = jnp.concatenate(
+        [sums[c * rank : (c + 1) * rank, c * rank : (c + 1) * rank] for c in range(checkpoints)], axis=1
+    )
+    for j in range(dp):
+        for k in range(tensor):
+            sent_ref[j * tensor + k] = grads[j * rows : (j + 1) * rows]
+
+
+def score_kernel(dp, checkpoints, terms_ref, queries_ref, listed_ref, sent_ref):
+    all_docs, rows, lanes = terms_ref.shape
+    rank = lanes // checkpoints
+    docs = all_docs // dp
+    parts = [terms_ref[:, r, :].astype(jnp.bfloat16) for r in range(rows)]
+    part = None
+    for c in range(checkpoints):
+        grads = jnp.concatenate([p[:, c * rank : (c + 1) * rank] for p in parts], axis=1)
+        term = lax.dot_general(grads, queries_ref[c], LAST, preferred_element_type=jnp.float32)
+        part = term if part is None else part + term
+    part = part * (1.0 / rank)
+    places = listed_ref.shape[0]
+    every = lax.broadcasted_iota(jnp.int32, part.shape, 0)
+    weight = jnp.zeros(part.shape, jnp.float32)
+    for k in range(places):
+        weight += jnp.where(listed_ref[k : k + 1, :] == every, 1.0 / places, 0.0)
+    own = jnp.sum(weight * part, axis=0, keepdims=True)
+    for j in range(dp):
+        sent_ref[j, 0:docs, :] = part[j * docs : (j + 1) * docs]
+        sent_ref[j, docs : docs + 1, :] = own
+
+
+def total_kernel(parts_ref, scores_ref, listed_ref):
+    docs = scores_ref.shape[0]
+    total = parts_ref[0]
+    for i in range(1, parts_ref.shape[0]):
+        total += parts_ref[i]
+    scores_ref[...] = total[:docs]
+    listed_ref[...] = total[docs:]
+
+
+def pair_body(dp, tensor, activations, out_grads, proj_in, proj_out, token_ids, queries, query_docs):
+    checkpoints, tokens, _ = activations.shape
+    rank = proj_in.shape[1]
+    docs, doc_len = token_ids.shape
+    rows = rank // dp
+    own_queries = queries.shape[1]
+    lanes = checkpoints * rank
+    steps = tokens // BLOCK
+    wide = activations.size + out_grads.size
+    f32 = jnp.float32
+
+    side = jax.ShapeDtypeStruct((doc_len, 2 * lanes), f32)
+    mine, theirs = pl.pallas_call(
+        functools.partial(project_kernel, doc_len),
+        in_specs=[HBM] * 4,
+        out_specs=[VMEM] * 2,
+        out_shape=[pltpu.VMEM(side.shape, f32)] * 2,
+        scratch_shapes=[
+            pltpu.VMEM(activations.shape, activations.dtype),
+            pltpu.VMEM(out_grads.shape, out_grads.dtype),
+            pltpu.VMEM(proj_in.shape[::-1], proj_in.dtype),
+            pltpu.VMEM(proj_out.shape[::-1], proj_out.dtype),
+            pltpu.SemaphoreType.DMA((steps, checkpoints)),
+            pltpu.SemaphoreType.DMA((steps, checkpoints)),
+            pltpu.SemaphoreType.DMA((2,)),
+        ],
+        compiler_params=pltpu.CompilerParams(vmem_limit_bytes=40 << 20),
+        cost_estimate=pl.CostEstimate(flops=2 * wide * rank, bytes_accessed=2 * wide, transcendentals=0),
+        name="project",
+    )(*(pltpu.with_memory_space_constraint(x, pltpu.HBM) for x in (activations, out_grads, proj_in.T, proj_out.T)))
+    other = lax.ppermute(theirs, "tensor", [(0, 1), (1, 0)])
+    sent = pl.pallas_call(
+        functools.partial(grad_kernel, dp, tensor, checkpoints),
+        in_specs=[VMEM] * 3,
+        out_specs=VMEM,
+        out_shape=jax.ShapeDtypeStruct((dp * tensor, rows, lanes), f32),
+        compiler_params=pltpu.CompilerParams(vmem_limit_bytes=4 << 20),
+        name="doc_grads",
+    )(token_ids, mine, other)
+    terms = lax.all_to_all(sent, ("dp", "tensor"), 0, 0, tiled=True)
+    parts = pl.pallas_call(
+        functools.partial(score_kernel, dp, checkpoints),
+        in_specs=[VMEM] * 3,
+        out_specs=VMEM,
+        out_shape=jax.ShapeDtypeStruct((dp, docs + 1, own_queries), f32),
+        compiler_params=pltpu.CompilerParams(vmem_limit_bytes=8 << 20),
+        name="partial_scores",
+    )(terms, queries, query_docs.T)
+    parts = lax.all_to_all(parts, "dp", 0, 0, tiled=True)
+    scores, listed = pl.pallas_call(
+        total_kernel,
+        in_specs=[VMEM],
+        out_specs=[VMEM] * 2,
+        out_shape=[jax.ShapeDtypeStruct((docs, own_queries), f32), jax.ShapeDtypeStruct((1, own_queries), f32)],
+        compiler_params=pltpu.CompilerParams(vmem_limit_bytes=4 << 20),
+        name="totals",
+    )(parts)
+    return scores, listed.reshape(own_queries)
 
 
 def sum_over_tensor(part, size):
@@ -12,7 +200,7 @@
     return lax.psum(part, "tensor")
 
 
-def body(dp, tensor, activations, out_grads, proj_in, proj_out, token_ids, queries, query_docs):
+def any_body(dp, tensor, activations, out_grads, proj_in, proj_out, token_ids, queries, query_docs):
     checkpoints = activations.shape[0]
     rank = proj_in.shape[1]
     docs, doc_len = token_ids.shape
@@ -50,6 +238,12 @@
 
 def solution(mesh):
     dp, tensor = mesh.shape["dp"], mesh.shape["tensor"]
+
+    def body(*arrays):
+        docs, doc_len = arrays[4].shape
+        paired = tensor == 2 and docs == 2 and doc_len % BLOCK == 0
+        return (pair_body if paired else any_body)(dp, tensor, *arrays)
+
     in_specs = (
         P(None, ("parts", "dp"), "tensor"),
         P(None, ("parts", "dp"), "tensor"),
@@ -61,7 +255,7 @@
     )
     out_specs = (P(("parts", "dp"), "tensor"), P(("parts", "tensor")))
     return jax.shard_map(
-        lambda *arrays: body(dp, tensor, *arrays),
+        body,
         mesh=mesh,
         in_specs=in_specs,
         out_specs=out_specs,

time: 47.3 us -> 40.8 us (0.86)
  matrix products: 18.2 us -> 0 us
  Pallas kernels: 0 us -> 14.5 us
  blocking collectives: 9.74 us -> 23.7 us
  starting transfers between devices: 7.54 us -> 0.52 us
  waiting for transfers between devices: 7.76 us -> 1.16 us
  local copies, waits for them, and re-layouts: 1.9 us -> 0.01 us
  other arithmetic: 1.12 us -> 0 us
    dot_general x4 -> x0, matrix products: 18.2 us -> none  [the longest x1 12.8 us: body(): jnp.einsum('ctf,fr->ctr', activations, proj_in, preferred_element_type=jn...]
    pallas_call x0 -> x4, Pallas kernels: none -> 14.5 us  [the longest x1 12.9 us: pair_body(): pl.pallas_call(functools.partial(project_kernel, doc_len), in_specs=[HBM]...]
    all_to_all x1 -> x2, blocking collectives: 9.74 us -> 23.7 us  [the longest x1 14 us: pair_body(): terms = lax.all_to_all(sent, ('dp', 'tensor'), 0, 0, tiled=True)]
    all_to_all x1 -> x0, waiting for transfers between devices: 7.76 us -> none  [body(): terms = lax.all_to_all(term, ('dp', 'tensor'), 0, 0, tiled=True)]
    all_to_all x1 -> x0, starting transfers between devices: 7.02 us -> none  [body(): terms = lax.all_to_all(term, ('dp', 'tensor'), 0, 0, tiled=True)]
    ppermute x1, waiting for transfers between devices: 0.01 us -> 1.16 us  [pair_body(): other = lax.ppermute(theirs, 'tensor', [(0, 1), (1, 0)])]
    broadcast_in_dim x3 -> x0, local copies, waits for them, and re-layouts: 0.68 us -> none  [the longest x2 0.66 us: body(): term = jnp.broadcast_to(term, (dp, tensor, checkpoints, rows, docs * rank))]
    div x2 -> x0, other arithmetic: 0.61 us -> none  [the longest x1 0.6 us: body(): return (total[:docs], total[docs] / query_docs.shape[1])]
  transfers between devices with their start and end apart: 2 -> 1, of which waited for: 1 -> 1; matrix products, arithmetic and copies ran while one was open for 28% -> 0% of each run, Pallas kernels for 0% -> 0%
where the time goes in v2:
time: 40.8 us; the launch traced here: 40.6 us
  blocking collectives  23.7 us (58%)
  Pallas kernels  14.5 us (36%)
  waiting for transfers between devices  1.16 us (3%)
  between operations  0.68 us (2%)
  starting transfers between devices  0.52 us (1%)
    all_to_all x1, blocking collectives, pair_body(): terms = lax.all_to_all(sent, ('dp', 'tensor'), 0, 0, tiled=True)  14 us
    pallas_call x1, Pallas kernels, pair_body(): pl.pallas_call(functools.partial(project_kernel, doc_len), in_specs=[HBM]...  12.9 us
    all_to_all x1, blocking collectives, pair_body(): parts = lax.all_to_all(parts, 'dp', 0, 0, tiled=True)  9.74 us
    ppermute x1, waiting for transfers between devices, pair_body(): other = lax.ppermute(theirs, 'tensor', [(0, 1), (1, 0)])  1.16 us
  transfers between devices with their start and end apart: 1, of which 1 were waited for; matrix products, arithmetic and copies ran while one was open for 0% of the time, Pallas kernels for 0%

profile of v2, /device:TPU:0, one launch (start us, length us, event | category | flops | bytes accessed | tf_op | source)
XLA Modules:
  0.0 40.6 jit_solution(2273434621870076437)
XLA Ops:
  0.6 0.0 copy-start.2
  0.6 0.0 copy-start
  0.7 0.0 copy-start.1
  0.7 12.9 %project.1 = (f32[256,256]{1,0:T(8,128)S(1)}, f32[256,256]{1,0:T(8,128)S(1)}) custom-call(bf16[2,512,12800]{2,1,0:T(8,128)(2,1)} %acts_ref.1, bf16[2,512,2560]{2,1,0:T(8,128)(2,1)} %outs_ref.1, bf16[64,12800]{1,0:T(8,128)(2,1)} %bitcast.5, bf16[64,2560]{1,0:T(8,128)(2,1)} %bitcast.6), custom_call_target="tpu_custom_call" | custom-call | flops 2013265920 | bytes 31457280 | tf_op jit(solution)/shard_map/project/pallas_call | solution.py:149
  13.6 0.5 %collective-permute-start = (f32[256,256]{1,0:T(8,128)S(1)}, f32[256,256]{1,0:T(8,128)S(1)}, u32[]{:S(2)}, u32[]{:S(2)}) collective-permute-start(f32[256,256]{1,0:T(8,128)S(1)} %get-tuple-element.7), channel_id=1, source_target_pairs={{0,1},{1,0},{2,3},{3,2},{4,5},{5,4},{6,7},{7,6},{8,9},{9,8},{10,11... | collective-permute-start | bytes 786440 | tf_op jit(solution)/shard_map/ppermute | solution.py:167
  14.1 1.2 %collective-permute-done.other_ref = f32[256,256]{1,0:T(8,128)S(1)} collective-permute-done((f32[256,256]{1,0:T(8,128)S(1)}, f32[256,256]{1,0:T(8,128)S(1)}, u32[]{:S(2)}, u32[]{:S(2)}) %collective-permute-start) | collective-permute-done | bytes 262176 | tf_op jit(solution)/shard_map/ppermute | solution.py:167
  15.3 0.0 copy-done.2
  15.3 0.3 doc_grads.1
  15.6 14.0 %all_to_all.10.terms_ref = f32[16,8,128]{2,1,0:T(8,128)S(1)} all-to-all(f32[16,8,128]{2,1,0:T(8,128)S(1)} %doc_grads.1), channel_id=1, replica_groups=mesh['parts'=2,'dp'=8,'tensor'=2] {'dp','tensor'}, dimensions={0} | all-to-all | bytes 131072 | tf_op jit(solution)/shard_map/all_to_all | solution.py:176
  29.6 0.0 copy-done
  29.6 0.0 copy-done.1
  29.6 0.7 %partial_scores.1 = f32[8,3,1024]{2,1,0:T(4,128)S(1)} custom-call(f32[16,8,128]{2,1,0:T(8,128)S(1)} %all_to_all.10.terms_ref, bf16[2,1024,512]{2,1,0:T(8,128)(2,1)S(1)} %copy-done, s32[8,1024]{1,0:T(8,128)S(1)} %bitcast.4), custom_call_target="tpu_custom_call" | custom-call | tf_op jit(solution)/shard_map/partial_scores/pallas_call | solution.py:177
  30.3 9.7 %all_to_all.11.parts_ref = f32[8,3,1024]{2,1,0:T(4,128)S(1)} all-to-all(f32[8,3,1024]{2,1,0:T(4,128)S(1)} %partial_scores.1), channel_id=1, replica_groups=mesh['parts'=2,'dp'=8,'tensor'=2] {'dp'}, dimensions={0} | all-to-all | bytes 196608 | tf_op jit(solution)/shard_map/all_to_all | solution.py:185
  40.0 0.6 %totals.1 = (f32[2,1024]{1,0:T(2,128)}, f32[1,1024]{1,0:T(1,128)}) custom-call(f32[8,3,1024]{2,1,0:T(4,128)S(1)} %all_to_all.11.parts_ref), custom_call_target="tpu_custom_call" | custom-call | tf_op jit(solution)/shard_map/totals/pallas_call | solution.py:186
Async XLA Ops:
  0.6 14.6 %copy-start.2 = (s32[2,256]{1,0:T(2,128)S(1)}, s32[2,256]{1,0:T(2,128)}, u32[]{:S(2)}) copy-start(s32[2,256]{1,0:T(2,128)} %ids_ref.1) | copy-start | bytes 6148
  0.6 28.9 %copy-start = (bf16[2,1024,512]{2,1,0:T(8,128)(2,1)S(1)}, bf16[2,1024,512]{2,1,0:T(8,128)(2,1)}, u32[]{:S(2)}) copy-start(bf16[2,1024,512]{2,1,0:T(8,128)(2,1)} %queries_ref.1) | copy-start | bytes 6291460
  0.7 28.9 %copy-start.1 = (s32[1024,8]{0,1:T(8,128)S(1)}, s32[1024,8]{0,1:T(8,128)}, u32[]{:S(2)}) copy-start(s32[1024,8]{0,1:T(8,128)} %param.13) | copy-start | bytes 98308
  13.6 1.7 %collective-permute-start = (f32[256,256]{1,0:T(8,128)S(1)}, f32[256,256]{1,0:T(8,128)S(1)}, u32[]{:S(2)}, u32[]{:S(2)}) collective-permute-start(f32[256,256]{1,0:T(8,128)S(1)} %get-tuple-element.7), channel_id=1, source_target_pairs={{0,1},{1,0},{2,3},{3,2},{4,5},{5,4},{6,7},{7,6},{8,9},{9,8},{10,11... | collective-permute-start | bytes 786440 | tf_op jit(solution)/shard_map/ppermute | solution.py:167

commit v3 on v2

--- a/solution.py
+++ b/solution.py
@@ -8,58 +8,82 @@
 from jax.sharding import PartitionSpec as P
 
 PAD = 151643
-BLOCK = 128
+BLOCK = 64
 VMEM = pl.BlockSpec(memory_space=pltpu.VMEM)
 HBM = pl.BlockSpec(memory_space=pltpu.HBM)
 LAST = (((1,), (1,)), ((), ()))
 
 
 def project_kernel(
-    doc_len, acts_ref, outs_ref, in_ref, out_ref, mine_ref, theirs_ref, acts, outs, infac, outfac, act_sems, out_sems, fac_sems
+    doc_len, acts_ref, outs_ref, in_ref, out_ref, ids_ref, queries_ref, listing_ref,
+    mine_ref, theirs_ref, near_queries_ref, near_listing_ref, acts, outs, infac, outfac, ids, act_sems, out_sems, sems
 ):
     checkpoints, tokens, _ = acts.shape
     rank = infac.shape[0]
     half = checkpoints * rank
-    steps = tokens // BLOCK
+    docs = tokens // doc_len
+    blocks = doc_len // BLOCK
     keeps = lax.axis_index("tensor")
 
-    def rows_of(i):
-        return pl.ds(pl.multiple_of(i * BLOCK, BLOCK), BLOCK)
-
-    def out_copy(i, c):
-        return pltpu.make_async_copy(outs_ref.at[c, rows_of(i)], outs.at[c, rows_of(i)], out_sems.at[i, c])
-
-    def act_copy(i, c):
-        return pltpu.make_async_copy(acts_ref.at[c, rows_of(i)], acts.at[c, rows_of(i)], act_sems.at[i, c])
-
-    out_fac_copy = pltpu.make_async_copy(out_ref, outfac, fac_sems.at[0])
-    in_fac_copy = pltpu.make_async_copy(in_ref, infac, fac_sems.at[1])
-
-    def start_outs(i, carry):
-        for c in range(checkpoints):
-            out_copy(i, c).start()
-        return carry
-
-    def start_acts(i, carry):
-        for c in range(checkpoints):
-            act_copy(i, c).start()
-        return carry
-
-    out_fac_copy.start()
-    lax.fori_loop(0, steps, start_outs, 0)
-    in_fac_copy.start()
-    lax.fori_loop(0, steps, start_acts, 0)
-
-    def project(i, copy, wide, factor, side):
-        for c in range(checkpoints):
-            copy(i, c).wait()
-        found = [
-            lax.dot_general(wide[c, rows_of(i)], factor[...], LAST, preferred_element_type=jnp.float32)
+    def place(i, first):
+        doc = jnp.where(i < first, 0, 1)
+        return doc, i - doc * first
+
+    def rows_of(doc, block):
+        return pl.ds(pl.multiple_of(doc * doc_len + block * BLOCK, BLOCK), BLOCK)
+
+    def doc_rows(doc):
+        return pl.ds(pl.multiple_of(doc * doc_len, doc_len), doc_len)
+
+    def out_copies(doc):
+        return [
+            pltpu.make_async_copy(outs_ref.at[c, doc_rows(doc)], outs.at[c, doc_rows(doc)], out_sems.at[doc, c])
             for c in range(checkpoints)
         ]
+
+    def act_copies(doc, block):
+        at = rows_of(doc, block)
+        return [
+            pltpu.make_async_copy(acts_ref.at[c, at], acts.at[c, at], act_sems.at[doc * blocks + block, c])
+            for c in range(checkpoints)
+        ]
+
+    def start(copies):
+        for copy in copies:
+            copy.start()
+
+    def wait(copies):
+        for copy in copies:
+            copy.wait()
+
+    out_fac_copy = pltpu.make_async_copy(out_ref, outfac, sems.at[0])
+    in_fac_copy = pltpu.make_async_copy(in_ref, infac, sems.at[1])
+    ids_copy = pltpu.make_async_copy(ids_ref, ids, sems.at[2])
+    late_copies = [
+        pltpu.make_async_copy(queries_ref, near_queries_ref, sems.at[3]),
+        pltpu.make_async_copy(listing_ref, near_listing_ref, sems.at[4]),
+    ]
+
+    ids_copy.start()
+    out_fac_copy.start()
+    for i in range(docs):
+        start(out_copies(i))
+    in_fac_copy.start()
+    start(act_copies(0, 0))
+    ids_copy.wait()
+    first, second = (
+        sum((ids[doc, block * BLOCK] != PAD).astype(jnp.int32) for block in range(blocks)) for doc in range(docs)
+    )
+
+    def start_acts(i, carry):
+        start(act_copies(*place(i, first)))
+        return carry
+
+    lax.fori_loop(1, first + second, start_acts, 0)
+    start(late_copies)
+
+    def put(doc, at, side, found):
         both = jnp.concatenate(found, axis=1)
-        doc = i // (doc_len // BLOCK)
-        at = pl.ds(pl.multiple_of(i * BLOCK - doc * doc_len, BLOCK), BLOCK)
 
         @pl.when(doc == keeps)
         def _():
@@ -69,18 +93,30 @@
         def _():
             theirs_ref[at, side * half : (side + 1) * half] = both
 
-    def out_step(i, carry):
-        project(i, out_copy, outs, outfac, 0)
+    def out_step(doc, carry):
+        wait(out_copies(doc))
+        found = [
+            lax.dot_general(outs[c, doc_rows(doc)], outfac[...], LAST, preferred_element_type=jnp.float32)
+            for c in range(checkpoints)
+        ]
+        put(doc, pl.ds(0, doc_len), 0, found)
         return carry
 
     def act_step(i, carry):
-        project(i, act_copy, acts, infac, 1)
+        doc, block = place(i, first)
+        wait(act_copies(doc, block))
+        found = [
+            lax.dot_general(acts[c, rows_of(doc, block)], infac[...], LAST, preferred_element_type=jnp.float32)
+            for c in range(checkpoints)
+        ]
+        put(doc, pl.ds(pl.multiple_of(block * BLOCK, BLOCK), BLOCK), 1, found)
         return carry
 
     out_fac_copy.wait()
-    lax.fori_loop(0, steps, out_step, 0)
+    lax.fori_loop(0, docs, out_step, 0)
     in_fac_copy.wait()
-    lax.fori_loop(0, steps, act_step, 0)
+    lax.fori_loop(0, first + second, act_step, 0)
+    wait(late_copies)
 
 
 def grad_kernel(dp, tensor, checkpoints, ids_ref, mine_ref, other_ref, sent_ref):
@@ -89,12 +125,15 @@
     rank = half // checkpoints
     rows = rank // dp
     ids = ids_ref[pl.ds(lax.axis_index("tensor"), 1), :]
-    keep = jnp.where(ids != PAD, doc_len**-0.5, 0.0)
+    kept = ids != PAD
+    places = lax.broadcasted_iota(jnp.int32, ids.shape, 1)
+    length = jnp.max(jnp.where(kept, places + 1, 0), axis=1, keepdims=True)
     both = mine_ref[...] + other_ref[...]
-    kept = both[:, :half].T * keep
+    out_side = jnp.where(kept, both[:, :half].T, 0.0)
+    in_side = jnp.where(lax.broadcasted_iota(jnp.int32, (doc_len, half), 0) < length, both[:, half:], 0.0)
     sums = jnp.dot(
-        kept, both[:, half:], precision=lax.Precision.HIGHEST, preferred_element_type=jnp.float32
-    )
+        out_side, in_side, precision=lax.Precision.HIGHEST, preferred_element_type=jnp.float32
+    ) * doc_len ** (-0.5)
     grads = jnp.concatenate(
         [sums[c * rank : (c + 1) * rank, c * rank : (c + 1) * rank] for c in range(checkpoints)], axis=1
     )
@@ -145,25 +184,31 @@
     wide = activations.size + out_grads.size
     f32 = jnp.float32
 
-    side = jax.ShapeDtypeStruct((doc_len, 2 * lanes), f32)
-    mine, theirs = pl.pallas_call(
+    near = (activations, out_grads, proj_in.T, proj_out.T, token_ids, queries, query_docs.T)
+    mine, theirs, near_queries, near_listing = pl.pallas_call(
         functools.partial(project_kernel, doc_len),
-        in_specs=[HBM] * 4,
-        out_specs=[VMEM] * 2,
-        out_shape=[pltpu.VMEM(side.shape, f32)] * 2,
+        in_specs=[HBM] * 7,
+        out_specs=[VMEM] * 4,
+        out_shape=[
+            pltpu.VMEM((doc_len, 2 * lanes), f32),
+            pltpu.VMEM((doc_len, 2 * lanes), f32),
+            pltpu.VMEM(queries.shape, queries.dtype),
+            pltpu.VMEM(query_docs.shape[::-1], query_docs.dtype),
+        ],
         scratch_shapes=[
             pltpu.VMEM(activations.shape, activations.dtype),
             pltpu.VMEM(out_grads.shape, out_grads.dtype),
             pltpu.VMEM(proj_in.shape[::-1], proj_in.dtype),
             pltpu.VMEM(proj_out.shape[::-1], proj_out.dtype),
+            pltpu.SMEM(token_ids.shape, token_ids.dtype),
             pltpu.SemaphoreType.DMA((steps, checkpoints)),
-            pltpu.SemaphoreType.DMA((steps, checkpoints)),
-            pltpu.SemaphoreType.DMA((2,)),
+            pltpu.SemaphoreType.DMA((docs, checkpoints)),
+            pltpu.SemaphoreType.DMA((5,)),
         ],
-        compiler_params=pltpu.CompilerParams(vmem_limit_bytes=40 << 20),
+        compiler_params=pltpu.CompilerParams(vmem_limit_bytes=44 << 20),
         cost_estimate=pl.CostEstimate(flops=2 * wide * rank, bytes_accessed=2 * wide, transcendentals=0),
         name="project",
-    )(*(pltpu.with_memory_space_constraint(x, pltpu.HBM) for x in (activations, out_grads, proj_in.T, proj_out.T)))
+    )(*(pltpu.with_memory_space_constraint(x, pltpu.HBM) for x in near))
     other = lax.ppermute(theirs, "tensor", [(0, 1), (1, 0)])
     sent = pl.pallas_call(
         functools.partial(grad_kernel, dp, tensor, checkpoints),
@@ -181,7 +226,7 @@
         out_shape=jax.ShapeDtypeStruct((dp, docs + 1, own_queries), f32),
         compiler_params=pltpu.CompilerParams(vmem_limit_bytes=8 << 20),
         name="partial_scores",
-    )(terms, queries, query_docs.T)
+    )(terms, near_queries, near_listing)
     parts = lax.all_to_all(parts, "dp", 0, 0, tiled=True)
     scores, listed = pl.pallas_call(
         total_kernel,

time: 40.8 us -> 39.4 us (0.966); the launches traced: 40.6 us -> 38.7 us
  Pallas kernels: 14.5 us -> 12.5 us
    pallas_call x1, Pallas kernels: 12.9 us -> 10.7 us  [pair_body(): pl.pallas_call(functools.partial(project_kernel, doc_len), in_specs=[HBM]...]
where the time goes in v3:
time: 39.4 us; the launch traced here: 38.7 us
  blocking collectives  23.9 us (61%)
  Pallas kernels  12.5 us (32%)
  waiting for transfers between devices  1.16 us (3%)
  between operations  0.66 us (2%)
  starting transfers between devices  0.53 us (1%)
    all_to_all x1, blocking collectives, pair_body(): terms = lax.all_to_all(sent, ('dp', 'tensor'), 0, 0, tiled=True)  14.1 us
    pallas_call x1, Pallas kernels, pair_body(): pl.pallas_call(functools.partial(project_kernel, doc_len), in_specs=[HBM]...  10.7 us
    all_to_all x1, blocking collectives, pair_body(): parts = lax.all_to_all(parts, 'dp', 0, 0, tiled=True)  9.74 us
    ppermute x1, waiting for transfers between devices, pair_body(): other = lax.ppermute(theirs, 'tensor', [(0, 1), (1, 0)])  1.16 us
  transfers between devices with their start and end apart: 1, of which 1 were waited for; matrix products, arithmetic and copies ran while one was open for 0% of the time, Pallas kernels for 0%

profile of v3, /device:TPU:0, one launch (start us, length us, event | category | flops | bytes accessed | tf_op | source)
XLA Modules:
  0.0 38.7 jit_solution(5018888710172997704)
XLA Ops:
  0.6 0.0 copy-start
  0.6 10.7 %project.1 = (f32[256,256]{1,0:T(8,128)S(1)}, f32[256,256]{1,0:T(8,128)S(1)}, bf16[2,1024,512]{2,1,0:T(8,128)(2,1)S(1)}, s32[8,1024]{1,0:T(8,128)S(1)}) custom-call(bf16[2,512,12800]{2,1,0:T(8,128)(2,1)} %acts_ref.1, bf16[2,512,2560]{2,1,0:T(8,128)(2,1)} %outs_ref.1, bf16[64,12800]{1,0:T(8,128)(2,1)} %bitcast.4, bf16[64,2560]{1,0:T(8,128)(2,1)} %bitcast.5, ...), custom_call_target="tpu_custom_call" | custom-call | flops 2013265920 | bytes 31457280 | tf_op jit(solution)/shard_map/project/pallas_call | solution.py:188
  11.4 0.5 %collective-permute-start = (f32[256,256]{1,0:T(8,128)S(1)}, f32[256,256]{1,0:T(8,128)S(1)}, u32[]{:S(2)}, u32[]{:S(2)}) collective-permute-start(f32[256,256]{1,0:T(8,128)S(1)} %get-tuple-element.9), channel_id=1, source_target_pairs={{0,1},{1,0},{2,3},{3,2},{4,5},{5,4},{6,7},{7,6},{8,9},{9,8},{10,11... | collective-permute-start | bytes 786440 | tf_op jit(solution)/shard_map/ppermute | solution.py:212
  11.9 1.2 %collective-permute-done.other_ref = f32[256,256]{1,0:T(8,128)S(1)} collective-permute-done((f32[256,256]{1,0:T(8,128)S(1)}, f32[256,256]{1,0:T(8,128)S(1)}, u32[]{:S(2)}, u32[]{:S(2)}) %collective-permute-start) | collective-permute-done | bytes 262176 | tf_op jit(solution)/shard_map/ppermute | solution.py:212
  13.1 0.0 copy-done
  13.1 0.5 %doc_grads.1 = f32[16,8,128]{2,1,0:T(8,128)S(1)} custom-call(s32[2,256]{1,0:T(2,128)S(1)} %copy-done, f32[256,256]{1,0:T(8,128)S(1)} %get-tuple-element.8.mine_ref, f32[256,256]{1,0:T(8,128)S(1)} %collective-permute-done.other_ref), custom_call_target="tpu_custom_call" | custom-call | tf_op jit(solution)/shard_map/doc_grads/pallas_call | solution.py:213
  13.5 14.1 %all_to_all.10.terms_ref = f32[16,8,128]{2,1,0:T(8,128)S(1)} all-to-all(f32[16,8,128]{2,1,0:T(8,128)S(1)} %doc_grads.1), channel_id=1, replica_groups=mesh['parts'=2,'dp'=8,'tensor'=2] {'dp','tensor'}, dimensions={0} | all-to-all | bytes 131072 | tf_op jit(solution)/shard_map/all_to_all | solution.py:221
  27.6 0.7 %partial_scores.1 = f32[8,3,1024]{2,1,0:T(4,128)S(1)} custom-call(f32[16,8,128]{2,1,0:T(8,128)S(1)} %all_to_all.10.terms_ref, bf16[2,1024,512]{2,1,0:T(8,128)(2,1)S(1)} %get-tuple-element.10.queries_ref, s32[8,1024]{1,0:T(8,128)S(1)} %get-tuple-element.11.listed_ref), custom_call_target="tpu_custom_call" | custom-call | tf_op jit(solution)/shard_map/partial_scores/pallas_call | solution.py:222
  28.3 9.7 %all_to_all.11.parts_ref = f32[8,3,1024]{2,1,0:T(4,128)S(1)} all-to-all(f32[8,3,1024]{2,1,0:T(4,128)S(1)} %partial_scores.1), channel_id=1, replica_groups=mesh['parts'=2,'dp'=8,'tensor'=2] {'dp'}, dimensions={0} | all-to-all | bytes 196608 | tf_op jit(solution)/shard_map/all_to_all | solution.py:230
  38.1 0.6 %totals.1 = (f32[2,1024]{1,0:T(2,128)}, f32[1,1024]{1,0:T(1,128)}) custom-call(f32[8,3,1024]{2,1,0:T(4,128)S(1)} %all_to_all.11.parts_ref), custom_call_target="tpu_custom_call" | custom-call | tf_op jit(solution)/shard_map/totals/pallas_call | solution.py:231
Async XLA Ops:
  0.6 12.4 %copy-start = (s32[2,256]{1,0:T(2,128)S(1)}, s32[2,256]{1,0:T(2,128)}, u32[]{:S(2)}) copy-start(s32[2,256]{1,0:T(2,128)} %ids_ref.3) | copy-start | bytes 6148
  11.4 1.7 %collective-permute-start = (f32[256,256]{1,0:T(8,128)S(1)}, f32[256,256]{1,0:T(8,128)S(1)}, u32[]{:S(2)}, u32[]{:S(2)}) collective-permute-start(f32[256,256]{1,0:T(8,128)S(1)} %get-tuple-element.9), channel_id=1, source_target_pairs={{0,1},{1,0},{2,3},{3,2},{4,5},{5,4},{6,7},{7,6},{8,9},{9,8},{10,11... | collective-permute-start | bytes 786440 | tf_op jit(solution)/shard_map/ppermute | solution.py:212

commit v4 on v3

--- a/solution.py
+++ b/solution.py
@@ -18,9 +18,7 @@
     doc_len, acts_ref, outs_ref, in_ref, out_ref, ids_ref, queries_ref, listing_ref,
     mine_ref, theirs_ref, near_queries_ref, near_listing_ref, acts, outs, infac, outfac, ids, act_sems, out_sems, sems
 ):
-    checkpoints, tokens, _ = acts.shape
-    rank = infac.shape[0]
-    half = checkpoints * rank
+    checkpoints, tokens, _ = acts_ref.shape
     docs = tokens // doc_len
     blocks = doc_len // BLOCK
     keeps = lax.axis_index("tensor")
@@ -32,21 +30,20 @@
     def rows_of(doc, block):
         return pl.ds(pl.multiple_of(doc * doc_len + block * BLOCK, BLOCK), BLOCK)
 
-    def doc_rows(doc):
-        return pl.ds(pl.multiple_of(doc * doc_len, doc_len), doc_len)
-
-    def out_copies(doc):
+    def copies_of(doc, block, wide_ref, wide, wide_sems):
+        slot = doc * blocks + block
         return [
-            pltpu.make_async_copy(outs_ref.at[c, doc_rows(doc)], outs.at[c, doc_rows(doc)], out_sems.at[doc, c])
+            pltpu.make_async_copy(
+                wide_ref.at[c, rows_of(doc, block)], wide.at[slot, pl.ds(c * BLOCK, BLOCK)], wide_sems.at[slot, c]
+            )
             for c in range(checkpoints)
         ]
 
+    def out_copies(doc, block):
+        return copies_of(doc, block, outs_ref, outs, out_sems)
+
     def act_copies(doc, block):
-        at = rows_of(doc, block)
-        return [
-            pltpu.make_async_copy(acts_ref.at[c, at], acts.at[c, at], act_sems.at[doc * blocks + block, c])
-            for c in range(checkpoints)
-        ]
+        return copies_of(doc, block, acts_ref, acts, act_sems)
 
     def start(copies):
         for copy in copies:
@@ -66,8 +63,7 @@
 
     ids_copy.start()
     out_fac_copy.start()
-    for i in range(docs):
-        start(out_copies(i))
+    start(out_copies(0, 0))
     in_fac_copy.start()
     start(act_copies(0, 0))
     ids_copy.wait()
@@ -76,46 +72,41 @@
     )
 
     def start_acts(i, carry):
+        start(out_copies(*place(i, first)))
         start(act_copies(*place(i, first)))
         return carry
 
     lax.fori_loop(1, first + second, start_acts, 0)
     start(late_copies)
 
-    def put(doc, at, side, found):
-        both = jnp.concatenate(found, axis=1)
+    mine_ref[...] = jnp.zeros_like(mine_ref)
+    theirs_ref[...] = jnp.zeros_like(theirs_ref)
+
+    def step(i, carry):
+        doc, block = place(i, first)
+        slot = doc * blocks + block
+        wait(out_copies(doc, block))
+        wait(act_copies(doc, block))
+        found = [
+            lax.dot_general(wide[slot], factor[...], LAST, preferred_element_type=jnp.float32)
+            for wide, factor in ((outs, outfac), (acts, infac))
+        ]
+        line = jnp.concatenate([x[c * BLOCK : (c + 1) * BLOCK] for x in found for c in range(checkpoints)], axis=1)
+        at = pl.ds(pl.multiple_of(block * BLOCK, BLOCK), BLOCK)
 
         @pl.when(doc == keeps)
         def _():
-            mine_ref[at, side * half : (side + 1) * half] = both
+            mine_ref[at] = line
 
         @pl.when(doc != keeps)
         def _():
-            theirs_ref[at, side * half : (side + 1) * half] = both
-
-    def out_step(doc, carry):
-        wait(out_copies(doc))
-        found = [
-            lax.dot_general(outs[c, doc_rows(doc)], outfac[...], LAST, preferred_element_type=jnp.float32)
-            for c in range(checkpoints)
-        ]
-        put(doc, pl.ds(0, doc_len), 0, found)
+            theirs_ref[at] = line
+
         return carry
 
-    def act_step(i, carry):
-        doc, block = place(i, first)
-        wait(act_copies(doc, block))
-        found = [
-            lax.dot_general(acts[c, rows_of(doc, block)], infac[...], LAST, preferred_element_type=jnp.float32)
-            for c in range(checkpoints)
-        ]
-        put(doc, pl.ds(pl.multiple_of(block * BLOCK, BLOCK), BLOCK), 1, found)
-        return carry
-
     out_fac_copy.wait()
-    lax.fori_loop(0, docs, out_step, 0)
     in_fac_copy.wait()
-    lax.fori_loop(0, first + second, act_step, 0)
+    lax.fori_loop(0, first + second, step, 0)
     wait(late_copies)
 
 
@@ -125,15 +116,14 @@
     rank = half // checkpoints
     rows = rank // dp
     ids = ids_ref[pl.ds(lax.axis_index("tensor"), 1), :]
-    kept = ids != PAD
-    places = lax.broadcasted_iota(jnp.int32, ids.shape, 1)
-    length = jnp.max(jnp.where(kept, places + 1, 0), axis=1, keepdims=True)
+    keep = jnp.where(ids != PAD, doc_len**-0.5, 0.0)
     both = mine_ref[...] + other_ref[...]
-    out_side = jnp.where(kept, both[:, :half].T, 0.0)
-    in_side = jnp.where(lax.broadcasted_iota(jnp.int32, (doc_len, half), 0) < length, both[:, half:], 0.0)
     sums = jnp.dot(
-        out_side, in_side, precision=lax.Precision.HIGHEST, preferred_element_type=jnp.float32
-    ) * doc_len ** (-0.5)
+        both[:, :half].T * keep,
+        both[:, half:],
+        precision=lax.Precision.HIGHEST,
+        preferred_element_type=jnp.float32,
+    )
     grads = jnp.concatenate(
         [sums[c * rank : (c + 1) * rank, c * rank : (c + 1) * rank] for c in range(checkpoints)], axis=1
     )
@@ -159,18 +149,29 @@
     for k in range(places):
         weight += jnp.where(listed_ref[k : k + 1, :] == every, 1.0 / places, 0.0)
     own = jnp.sum(weight * part, axis=0, keepdims=True)
-    for j in range(dp):
-        sent_ref[j, 0:docs, :] = part[j * docs : (j + 1) * docs]
-        sent_ref[j, docs : docs + 1, :] = own
+    lines = part.shape[1] // 128
+    for line in range(lines):
+        at = slice(line * 128, (line + 1) * 128)
+        for j in range(dp):
+            for doc in range(docs):
+                n = j * docs + doc
+                sent_ref[j, pl.ds(doc * lines + line, 1), :] = part[n : n + 1, at]
+            sent_ref[j, pl.ds(docs * lines + line, 1), :] = own[:, at]
 
 
 def total_kernel(parts_ref, scores_ref, listed_ref):
-    docs = scores_ref.shape[0]
+    docs, columns = scores_ref.shape
+    lines = columns // 128
     total = parts_ref[0]
     for i in range(1, parts_ref.shape[0]):
         total += parts_ref[i]
-    scores_ref[...] = total[:docs]
-    listed_ref[...] = total[docs:]
+    for line in range(lines):
+        at = slice(line * 128, (line + 1) * 128)
+        for doc in range(docs):
+            n = doc * lines + line
+            scores_ref[doc : doc + 1, at] = total[n : n + 1]
+        n = docs * lines + line
+        listed_ref[:, at] = total[n : n + 1]
 
 
 def pair_body(dp, tensor, activations, out_grads, proj_in, proj_out, token_ids, queries, query_docs):
@@ -196,13 +197,13 @@
             pltpu.VMEM(query_docs.shape[::-1], query_docs.dtype),
         ],
         scratch_shapes=[
-            pltpu.VMEM(activations.shape, activations.dtype),
-            pltpu.VMEM(out_grads.shape, out_grads.dtype),
+            pltpu.VMEM((tokens // BLOCK, checkpoints * BLOCK, activations.shape[2]), activations.dtype),
+            pltpu.VMEM((tokens // BLOCK, checkpoints * BLOCK, out_grads.shape[2]), out_grads.dtype),
             pltpu.VMEM(proj_in.shape[::-1], proj_in.dtype),
             pltpu.VMEM(proj_out.shape[::-1], proj_out.dtype),
             pltpu.SMEM(token_ids.shape, token_ids.dtype),
             pltpu.SemaphoreType.DMA((steps, checkpoints)),
-            pltpu.SemaphoreType.DMA((docs, checkpoints)),
+            pltpu.SemaphoreType.DMA((steps, checkpoints)),
             pltpu.SemaphoreType.DMA((5,)),
         ],
         compiler_params=pltpu.CompilerParams(vmem_limit_bytes=44 << 20),
@@ -223,7 +224,7 @@
         functools.partial(score_kernel, dp, checkpoints),
         in_specs=[VMEM] * 3,
         out_specs=VMEM,
-        out_shape=jax.ShapeDtypeStruct((dp, docs + 1, own_queries), f32),
+        out_shape=jax.ShapeDtypeStruct((dp, (docs + 1) * own_queries // 128, 128), f32),
         compiler_params=pltpu.CompilerParams(vmem_limit_bytes=8 << 20),
         name="partial_scores",
     )(terms, near_queries, near_listing)
@@ -286,7 +287,7 @@
 
     def body(*arrays):
         docs, doc_len = arrays[4].shape
-        paired = tensor == 2 and docs == 2 and doc_len % BLOCK == 0
+        paired = tensor == 2 and docs == 2 and doc_len % BLOCK == 0 and arrays[5].shape[1] % 128 == 0
         return (pair_body if paired else any_body)(dp, tensor, *arrays)
 
     in_specs = (

time: 39.4 us -> 39.8 us (1.010); the launches traced: 38.7 us -> 39.6 us
  blocking collectives: 23.9 us -> 26.3 us
  Pallas kernels: 12.5 us -> 11 us
    all_to_all x1, blocking collectives: 14.1 us -> 16.8 us  [pair_body(): terms = lax.all_to_all(sent, ('dp', 'tensor'), 0, 0, tiled=True)]
    pallas_call x1, Pallas kernels: 10.7 us -> 9.35 us  [pair_body(): pl.pallas_call(functools.partial(project_kernel, doc_len), in_specs=[HBM]...]
where the time goes in v4:
time: 39.8 us; the launch traced here: 39.6 us
  blocking collectives  26.3 us (66%)
  Pallas kernels  11 us (28%)
  waiting for transfers between devices  1.16 us (3%)
  between operations  0.66 us (2%)
  starting transfers between devices  0.52 us (1%)
    all_to_all x1, blocking collectives, pair_body(): terms = lax.all_to_all(sent, ('dp', 'tensor'), 0, 0, tiled=True)  16.8 us
    all_to_all x1, blocking collectives, pair_body(): parts = lax.all_to_all(parts, 'dp', 0, 0, tiled=True)  9.51 us
    pallas_call x1, Pallas kernels, pair_body(): pl.pallas_call(functools.partial(project_kernel, doc_len), in_specs=[HBM]...  9.35 us
    ppermute x1, waiting for transfers between devices, pair_body(): other = lax.ppermute(theirs, 'tensor', [(0, 1), (1, 0)])  1.16 us
  transfers between devices with their start and end apart: 1, of which 1 were waited for; matrix products, arithmetic and copies ran while one was open for 0% of the time, Pallas kernels for 0%

profile of v4, /device:TPU:0, one launch (start us, length us, event | category | flops | bytes accessed | tf_op | source)
XLA Modules:
  0.0 39.6 jit_solution(5533718658072451725)
XLA Ops:
  0.6 0.0 copy-start
  0.6 9.3 %project.1 = (f32[256,256]{1,0:T(8,128)S(1)}, f32[256,256]{1,0:T(8,128)S(1)}, bf16[2,1024,512]{2,1,0:T(8,128)(2,1)S(1)}, s32[8,1024]{1,0:T(8,128)S(1)}) custom-call(bf16[2,512,12800]{2,1,0:T(8,128)(2,1)} %acts_ref.1, bf16[2,512,2560]{2,1,0:T(8,128)(2,1)} %outs_ref.1, bf16[64,12800]{1,0:T(8,128)(2,1)} %bitcast.4, bf16[64,2560]{1,0:T(8,128)(2,1)} %bitcast.5, ...), custom_call_target="tpu_custom_call" | custom-call | flops 2013265920 | bytes 31457280 | tf_op jit(solution)/shard_map/project/pallas_call | solution.py:189
  10.0 0.5 %collective-permute-start = (f32[256,256]{1,0:T(8,128)S(1)}, f32[256,256]{1,0:T(8,128)S(1)}, u32[]{:S(2)}, u32[]{:S(2)}) collective-permute-start(f32[256,256]{1,0:T(8,128)S(1)} %get-tuple-element.9), channel_id=1, source_target_pairs={{0,1},{1,0},{2,3},{3,2},{4,5},{5,4},{6,7},{7,6},{8,9},{9,8},{10,11... | collective-permute-start | bytes 786440 | tf_op jit(solution)/shard_map/ppermute | solution.py:213
  10.5 1.2 %collective-permute-done.other_ref = f32[256,256]{1,0:T(8,128)S(1)} collective-permute-done((f32[256,256]{1,0:T(8,128)S(1)}, f32[256,256]{1,0:T(8,128)S(1)}, u32[]{:S(2)}, u32[]{:S(2)}) %collective-permute-start) | collective-permute-done | bytes 262176 | tf_op jit(solution)/shard_map/ppermute | solution.py:213
  11.7 0.0 copy-done
  11.7 0.3 doc_grads.1
  12.0 16.8 %all_to_all.10.terms_ref = f32[16,8,128]{2,1,0:T(8,128)S(1)} all-to-all(f32[16,8,128]{2,1,0:T(8,128)S(1)} %doc_grads.1), channel_id=1, replica_groups=mesh['parts'=2,'dp'=8,'tensor'=2] {'dp','tensor'}, dimensions={0} | all-to-all | bytes 131072 | tf_op jit(solution)/shard_map/all_to_all | solution.py:222
  28.8 0.7 %partial_scores.1 = f32[8,24,128]{2,1,0:T(8,128)S(1)} custom-call(f32[16,8,128]{2,1,0:T(8,128)S(1)} %all_to_all.10.terms_ref, bf16[2,1024,512]{2,1,0:T(8,128)(2,1)S(1)} %get-tuple-element.10.queries_ref, s32[8,1024]{1,0:T(8,128)S(1)} %get-tuple-element.11.listed_ref), custom_call_target="tpu_custom_call" | custom-call | tf_op jit(solution)/shard_map/partial_scores/pallas_call | solution.py:223
  29.5 9.5 %all_to_all.11.parts_ref = f32[8,24,128]{2,1,0:T(8,128)S(1)} all-to-all(f32[8,24,128]{2,1,0:T(8,128)S(1)} %partial_scores.1), channel_id=1, replica_groups=mesh['parts'=2,'dp'=8,'tensor'=2] {'dp'}, dimensions={0} | all-to-all | bytes 196608 | tf_op jit(solution)/shard_map/all_to_all | solution.py:231
  39.0 0.6 %totals.1 = (f32[2,1024]{1,0:T(2,128)}, f32[1,1024]{1,0:T(1,128)}) custom-call(f32[8,24,128]{2,1,0:T(8,128)S(1)} %all_to_all.11.parts_ref), custom_call_target="tpu_custom_call" | custom-call | tf_op jit(solution)/shard_map/totals/pallas_call | solution.py:232
Async XLA Ops:
  0.6 11.0 %copy-start = (s32[2,256]{1,0:T(2,128)S(1)}, s32[2,256]{1,0:T(2,128)}, u32[]{:S(2)}) copy-start(s32[2,256]{1,0:T(2,128)} %ids_ref.3) | copy-start | bytes 6148
  10.0 1.7 %collective-permute-start = (f32[256,256]{1,0:T(8,128)S(1)}, f32[256,256]{1,0:T(8,128)S(1)}, u32[]{:S(2)}, u32[]{:S(2)}) collective-permute-start(f32[256,256]{1,0:T(8,128)S(1)} %get-tuple-element.9), channel_id=1, source_target_pairs={{0,1},{1,0},{2,3},{3,2},{4,5},{5,4},{6,7},{7,6},{8,9},{9,8},{10,11... | collective-permute-start | bytes 786440 | tf_op jit(solution)/shard_map/ppermute | solution.py:213
